TPU v7x, 32 devices: a whole 2x2x4 slice. The times are simulated.
32 devices in a mesh: tile: 16 (over z, y, core), layer: 2 (over x).
Axes of the slice: x: 2, y: 2, z: 4, core: 2. Of those that a mesh axis runs over, the one named last changes fastest.
Arguments:
- ensemble: float32 [64, 8, 8192], P(None, 'layer', 'tile'), may hold values from -6 to 6
- diff_x: float32 [8, 8192], P('layer', 'tile'), may hold values from 0.04 to 0.2
- diff_z: float32 [8, 8192], P('layer', 'tile'), may hold values from 0.04 to 0.2
- cour_x: float32 [8, 8192], P('layer', 'tile'), may hold values from -0.4 to 0.4
- cour_z: float32 [8, 8192], P('layer', 'tile'), may hold values from -0.4 to 0.4
- obs_cell: int32 [4, 512], replicated, may hold values from 0 to 65535
- obs_radius: int32 [4, 512], replicated, may hold values from 2048 to 8192
- obs_value: float32 [4, 512], replicated, may hold values from -6 to 6
- obs_var: float32 [4, 512], replicated, may hold values from 0.1 to 1
Outputs:
- posterior: float32 [64, 8, 8192], P(None, 'layer', 'tile')
Inputs may be any that keep to these rules, and one draw needn't show every extreme that they name: `obs_cell`: cells are drawn independently over the whole grid; two observations may share a cell.
All inputs are finite; a program needn't handle non-finite values.
Results may differ from a plain program's by a relative error of at most 0.00019.
Values sent between devices are 32-bit elements; how exact they have to be, the bound alone decides.
A program may use at most 64 MiB of HBM per device.

v0:
```python
import jax
import jax.numpy as jnp
from jax import lax
from jax.sharding import PartitionSpec as P


def extended(cells, sides, width):
    for axis, dim in sides:
        count = lax.axis_size(axis)
        ends = count - 1
        head = lax.slice_in_dim(cells, 0, width, axis=dim)
        tail = lax.slice_in_dim(cells, cells.shape[dim] - width, cells.shape[dim], axis=dim)
        cells = jnp.concatenate(
            [
                lax.ppermute(tail, axis, [(i, (i + 1) % count) for i in range(ends)]),
                cells,
                lax.ppermute(head, axis, [((i + 1) % count, i) for i in range(ends)]),
            ],
            axis=dim,
        )
    return cells


def increments(prior, value, variance):
    members = prior.shape[1]
    ymean = jnp.mean(prior, axis=1)
    anomaly = prior - ymean[:, None]
    spread = jnp.sum(anomaly * anomaly, axis=1) / (members - 1) + 1e-06
    shrink = variance / (spread + variance)
    postmean = spread * shrink * (ymean / spread + value / variance)
    delta = (postmean - ymean)[:, None] + (jnp.sqrt(shrink) - 1.0)[:, None] * anomaly
    factor = 1.0 / ((members - 1) * spread)
    return (anomaly, delta, factor)


def taper(positions, centres, radius):
    dist = jnp.abs(positions[None, :] - centres[:, None]).astype(jnp.float32)
    frac = jnp.maximum(1.0 - dist / radius[:, None].astype(jnp.float32), 0.0)
    return frac * frac


def pick_local(flat, cells, first_layer, first_col, depth, width, total_cols):
    rows = cells // total_cols - first_layer
    cols = cells % total_cols - first_col
    inside = (rows >= 0) & (rows < depth) & (cols >= 0) & (cols < width)
    index = jnp.where(inside, rows * width + cols, 0)
    values = jnp.take(flat, index, axis=1).T
    return jnp.where(inside[:, None], values, 0.0)


def gather_prior(picked):
    return lax.psum(picked, ("tile", "layer"))


def regress(state, anomaly, delta, weight):
    members, depth, width = state.shape
    count = anomaly.shape[0]
    xmean = jnp.mean(state, axis=0)
    deviation = (state - xmean[None]).reshape(members, depth * width)
    block = min(128, count)
    change = jnp.zeros((members, depth * width), jnp.float32)
    for start in range(0, count, block):
        cov = jnp.dot(anomaly[start : start + block], deviation, precision=lax.Precision.HIGHEST)
        gain = (
            cov.reshape(block, depth, width) * weight[start : start + block][:, None, :]
        ).reshape(block, depth * width)
        change = change + jnp.dot(
            delta[start : start + block].T, gain, precision=lax.Precision.HIGHEST
        )
    return state + change.reshape(members, depth, width)


def shards(ensemble, diff_x, diff_z, cour_x, cour_z, obs_cell, obs_radius, obs_value, obs_var):
    members, depth, width = ensemble.shape
    total_cols = width * lax.axis_size("tile")
    first_col = lax.axis_index("tile") * width
    first_layer = lax.axis_index("layer") * depth
    padded = extended(ensemble, (("tile", 2), ("layer", 1)), 1)
    centre = padded[:, 1:-1, 1:-1]
    upper = padded[:, :-2, 1:-1]
    lower = padded[:, 2:, 1:-1]
    west = padded[:, 1:-1, :-2]
    east = padded[:, 1:-1, 2:]
    state = (
        centre
        + diff_z * (upper - 2.0 * centre + lower)
        + diff_x * (west - 2.0 * centre + east)
        - 0.5 * cour_z * (lower - upper)
        - 0.5 * cour_x * (east - west)
    )
    positions = first_col + jnp.arange(width, dtype=jnp.int32)
    batches, count = obs_cell.shape
    for batch in range(batches):
        cells = obs_cell[batch]
        flat = state.reshape(members, depth * width)
        prior = gather_prior(
            pick_local(flat, cells, first_layer, first_col, depth, width, total_cols)
        )
        anomaly, delta, factor = increments(prior, obs_value[batch], obs_var[batch])
        weight = taper(positions, cells % total_cols, obs_radius[batch]) * factor[:, None]
        state = regress(state, anomaly, delta, weight)
    return state


def solution(mesh):
    in_specs = (
        P(None, "layer", "tile"),
        P("layer", "tile"),
        P("layer", "tile"),
        P("layer", "tile"),
        P("layer", "tile"),
        P(),
        P(),
        P(),
        P(),
    )
    out_specs = P(None, "layer", "tile")
    return jax.shard_map(shards, mesh=mesh, in_specs=in_specs, out_specs=out_specs, check_vma=False)
```

profile of v0, /device:TPU:0, one launch (start us, length us, event | category | flops | bytes accessed | tf_op | source)
XLA Modules:
  0.0 607.9 jit_solution(5944438097676178219)
XLA Ops:
  6.5 1.2 copy.114
  7.9 1.3 collective-permute-start.1
  9.2 3.0 collective-permute-start
  18.0 1.3 collective-permute-start.3
  19.3 4.9 collective-permute-start.2
  24.8 1.1 collective-permute-done.3
  26.0 1.8 collective-permute-done.2
  28.6 1.0 gather_fusion
  30.5 125.8 %all-reduce.5.cloned.1.call-done = f32[512,64]{0,1:T(8,128)} async-done(((f32[512,64]{0,1:T(8,128)}), f32[512,64]{0,1:T(8,128)}) %all-reduce.5.cloned.1.call-update) | async-done | bytes 131088 | tf_op jit(solution)/shard_map/psum | solution.py:52
  156.4 1.0 reduce_sum.108
  158.5 1.0 convolution_multiply_fusion.15
  159.9 1.0 convolution_multiply_fusion.14
  160.9 1.3 copy.123
  162.3 1.0 convolution_multiply_fusion.13
  163.3 1.3 copy.125
  164.6 1.0 convolution_multiply_fusion.12
  165.6 1.3 copy.127
  167.0 1.2 fusion.54
  168.3 1.2 convolution_add_fusion.11
  169.5 1.3 convolution_add_fusion.10
  170.8 1.2 convolution_add_fusion.9
  172.8 1.0 gather_fusion.1
  175.8 121.1 %all-reduce.7.cloned.1.call-done = f32[512,64]{0,1:T(8,128)} async-done(((f32[512,64]{0,1:T(8,128)}), f32[512,64]{0,1:T(8,128)}) %all-reduce.7.cloned.1.call-update) | async-done | bytes 131088 | tf_op jit(solution)/shard_map/psum | solution.py:52
  296.9 1.0 reduce_sum.111
  300.6 1.0 convolution_multiply_fusion.11
  302.0 2.0 convolution_multiply_fusion.10
  303.9 1.3 copy.135
  305.3 1.0 convolution_multiply_fusion.9
  306.3 1.3 copy.137
  307.6 1.0 convolution_multiply_fusion.8
  308.6 1.3 copy.139
  310.0 1.2 fusion.49
  311.3 1.3 convolution_add_fusion.8
  312.5 1.2 convolution_add_fusion.7
  313.8 1.2 convolution_add_fusion.6
  315.8 1.0 gather_fusion.2
  318.6 121.3 %all-reduce.9.cloned.1.call-done = f32[512,64]{0,1:T(8,128)} async-done(((f32[512,64]{0,1:T(8,128)}), f32[512,64]{0,1:T(8,128)}) %all-reduce.9.cloned.1.call-update) | async-done | bytes 131088 | tf_op jit(solution)/shard_map/psum | solution.py:52
  439.9 1.0 reduce_sum.114
  443.5 1.0 convolution_multiply_fusion.7
  444.8 1.0 convolution_multiply_fusion.6
  445.9 1.3 copy.147
  447.2 1.0 convolution_multiply_fusion.5
  448.2 1.3 copy.149
  449.5 1.0 convolution_multiply_fusion.4
  450.6 1.3 copy.151
  452.0 1.2 fusion.44
  453.2 1.2 convolution_add_fusion.5
  454.5 1.3 convolution_add_fusion.4
  455.7 1.2 convolution_add_fusion.3
  457.4 1.2 gather_fusion.3
  460.2 121.6 %all-reduce.11.cloned.1.call-done = f32[512,64]{0,1:T(8,128)} async-done(((f32[512,64]{0,1:T(8,128)}), f32[512,64]{0,1:T(8,128)}) %all-reduce.11.cloned.1.call-update) | async-done | bytes 131088 | tf_op jit(solution)/shard_map/psum | solution.py:52
  581.8 1.0 reduce_sum.117
  585.5 1.0 convolution_multiply_fusion.3
  586.8 2.0 convolution_multiply_fusion.2
  588.8 1.3 copy.159
  590.1 1.0 convolution_multiply_fusion.1
  591.2 1.3 copy.161
  592.5 1.0 convolution_multiply_fusion
  593.5 1.3 copy.163
  594.9 1.2 fusion.39
  596.1 1.3 convolution_add_fusion.2
  597.4 1.2 convolution_add_fusion.1
  598.7 1.2 convolution_add_fusion
  600.0 1.1 copy.165
  (172 shorter events, 25.7 us)
Async XLA Ops:
  6.5 149.8 %all-reduce.5.cloned.1.call-start = ((), (), s32[]{:S(2)}) async-start(), calls=%async_computation | async-start | bytes 262144 | tf_op jit(solution)/shard_map/psum | solution.py:52
  7.8 4.4 copy-start.30
  7.9 10.0 %collective-permute-start.1 = (f32[64,4,1]{2,0,1:T(8,128)S(1)}, f32[64,4,1]{2,0,1:T(8,128)S(1)}, u32[]{:S(2)}, u32[]{:S(2)}) collective-permute-start(f32[64,4,1]{2,0,1:T(8,128)S(1)} %get-tuple-element.53), channel_id=1, source_target_pairs={{2,0},{4,2},{6,4},{8,6},{10,8},{12,10},{14,12},{16,14},{18,16},{20... | collective-permute-start | bytes 3080 | tf_op jit(solution)/shard_map/ppermute | solution.py:17
  9.2 8.7 %collective-permute-start = (f32[64,4,1]{2,0,1:T(8,128)S(1)}, f32[64,4,1]{2,0,1:T(8,128)S(1)}, u32[]{:S(2)}, u32[]{:S(2)}) collective-permute-start(f32[64,4,1]{2,0,1:T(8,128)S(1)} %get-tuple-element.52), channel_id=1, source_target_pairs={{0,2},{2,4},{4,6},{6,8},{8,10},{10,12},{12,14},{14,16},{16,18},{18... | collective-permute-start | bytes 3080 | tf_op jit(solution)/shard_map/ppermute | solution.py:15
  13.9 1.2 copy-start.31
  15.2 0.7 copy-start.32
  15.8 0.7 copy-start.33
  16.5 0.7 copy-start.34
  16.5 0.7 copy-start.35
  18.0 7.9 %collective-permute-start.3 = (f32[64,1,514]{2,0,1:T(8,128)S(1)}, f32[64,1,514]{2,0,1:T(8,128)S(1)}, u32[]{:S(2)}, u32[]{:S(2)}) collective-permute-start(f32[64,1,514]{2,0,1:T(8,128)S(1)} %get-tuple-element.51), channel_id=1, source_target_pairs={{1,0},{3,2},{5,4},{7,6},{9,8},{11,10},{13,12},{15,14},{17,16},{19,... | collective-permute-start | bytes 394760 | tf_op jit(solution)/shard_map/ppermute | solution.py:17
  19.3 8.4 %collective-permute-start.2 = (f32[64,1,514]{2,0,1:T(8,128)S(1)}, f32[64,1,514]{2,0,1:T(8,128)S(1)}, u32[]{:S(2)}, u32[]{:S(2)}) collective-permute-start(f32[64,1,514]{2,0,1:T(8,128)S(1)} %get-tuple-element.50), channel_id=1, source_target_pairs={{0,1},{2,3},{4,5},{6,7},{8,9},{10,11},{12,13},{14,15},{16,17},{18,... | collective-permute-start | bytes 394760 | tf_op jit(solution)/shard_map/ppermute | solution.py:15
  24.2 3.5 copy-start.18
  24.2 3.5 copy-start.19
  30.5 266.4 %all-reduce.7.cloned.1.call-start = ((), (), s32[]{:S(2)}) async-start(), calls=%async_computation.1 | async-start | bytes 262144 | tf_op jit(solution)/shard_map/psum | solution.py:52
  156.4 1.0 copy-start.12
  165.6 1.4 copy-start.20
  165.6 1.4 copy-start.21
  167.0 1.3 copy-start
  168.3 1.3 copy-start.4
  169.5 1.3 copy-start.8
  172.2 0.7 copy-start.17
  174.0 0.6 copy-start.46
  174.0 0.6 copy-start.47
  175.3 264.6 %all-reduce.9.cloned.1.call-start = ((), (), s32[]{:S(2)}) async-start(), calls=%async_computation.2 | async-start | bytes 262144 | tf_op jit(solution)/shard_map/psum | solution.py:52
  296.9 1.0 copy-start.13
  298.0 0.7 copy-start.41
  298.0 0.7 copy-start.40
  298.7 0.7 copy-start.29
  298.7 0.7 copy-start.26
  310.0 1.3 copy-start.1
  311.2 1.3 copy-start.5
  312.5 1.3 copy-start.9
  315.1 0.7 copy-start.16
  317.0 0.7 copy-start.44
  317.0 0.7 copy-start.45
  318.4 263.4 %all-reduce.11.cloned.1.call-start = ((), (), s32[]{:S(2)}) async-start(), calls=%async_computation.3 | async-start | bytes 262144 | tf_op jit(solution)/shard_map/psum | solution.py:52
  439.9 1.0 copy-start.14
  441.0 0.7 copy-start.39
  441.0 0.7 copy-start.38
  442.3 0.7 copy-start.28
  442.3 0.7 copy-start.25
  450.6 1.4 copy-start.22
  450.6 1.4 copy-start.23
  451.9 1.3 copy-start.2
  453.2 1.3 copy-start.6
  454.5 1.3 copy-start.10
  458.8 0.6 copy-start.42
  458.8 0.7 copy-start.43
  581.8 1.0 copy-start.15
  582.9 0.7 copy-start.37
  582.9 0.7 copy-start.36
  583.6 0.7 copy-start.27
  583.6 0.7 copy-start.24
  594.8 1.3 copy-start.3
  596.1 1.3 copy-start.7
  597.4 1.3 copy-start.11
Sparse Core Ops, SparseCore 0:
  30.6 125.7 all-reduce.4
  175.4 121.4 all-reduce.6
  318.5 121.4 all-reduce.8
  460.3 121.4 all-reduce.10
where the time goes:
time: 617 us; the launch traced here: 608 us
  waiting for transfers between devices  493 us (80%)
  matrix products  38.2 us (6%)
  local copies, waits for them, and re-layouts  35.8 us (6%)
  other arithmetic  15.7 us (3%)
  between operations  14.2 us (2%)
  starting transfers between devices  11.2 us (2%)
    psum x4, waiting for transfers between devices, gather_prior(): return lax.psum(picked, ('tile', 'layer'))  490 us
    dot_general x16, matrix products, regress(): jnp.dot(delta[start:start + block].T, gain, precision=lax.Precision.HIGHEST)  20 us
    dot_general x16, matrix products, regress(): jnp.dot(anomaly[start:start + block], deviation, precision=lax.Precision....  18.2 us
    mul x16, local copies, waits for them, and re-layouts, regress(): cov.reshape(block, depth, width) * weight[start:start + block][:, None, :]  17.2 us
  transfers between devices with their start and end apart: 8, of which 6 were waited for; matrix products, arithmetic and copies ran while one was open for 1% of the time, Pallas kernels for 0%

commit v1 on v0

--- a/solution.py
+++ b/solution.py
@@ -49,7 +49,7 @@
 
 
 def gather_prior(picked):
-    return lax.psum(picked, ("tile", "layer"))
+    return lax.psum(lax.psum(picked, "layer"), "tile")
 
 
 def regress(state, anomaly, delta, weight):

time: 617 us -> 582 us (0.943)
  waiting for transfers between devices: 493 us -> 456 us
    psum x4 -> x8, waiting for transfers between devices: 490 us -> 453 us  [gather_prior(): return lax.psum(lax.psum(picked, 'layer'), 'tile')]
  transfers between devices with their start and end apart: 8 -> 12, of which waited for: 6 -> 10; matrix products, arithmetic and copies ran while one was open for 1% -> 1% of each run, Pallas kernels for 0% -> 0%
where the time goes in v1:
time: 582 us; the launch traced here: 572 us
  waiting for transfers between devices  456 us (78%)
  matrix products  38.2 us (7%)
  local copies, waits for them, and re-layouts  37.4 us (6%)
  between operations  14.6 us (3%)
  other arithmetic  14 us (2%)
  starting transfers between devices  11.6 us (2%)
    psum x8, waiting for transfers between devices, gather_prior(): return lax.psum(lax.psum(picked, 'layer'), 'tile')  453 us
    dot_general x16, matrix products, regress(): jnp.dot(delta[start:start + block].T, gain, precision=lax.Precision.HIGHEST)  20 us
    dot_general x16, matrix products, regress(): jnp.dot(anomaly[start:start + block], deviation, precision=lax.Precision....  18.2 us
    mul x16, local copies, waits for them, and re-layouts, regress(): cov.reshape(block, depth, width) * weight[start:start + block][:, None, :]  17.2 us
  transfers between devices with their start and end apart: 12, of which 10 were waited for; matrix products, arithmetic and copies ran while one was open for 1% of the time, Pallas kernels for 0%

profile of v1, /device:TPU:0, one launch (start us, length us, event | category | flops | bytes accessed | tf_op | source)
XLA Modules:
  0.0 571.5 jit_solution(6593025319970472767)
XLA Ops:
  6.5 1.2 copy.114
  7.9 1.3 collective-permute-start.1
  9.2 3.0 collective-permute-start
  15.8 1.3 collective-permute-start.3
  17.1 4.9 collective-permute-start.2
  22.7 1.1 collective-permute-done.3
  23.7 1.8 collective-permute-done.2
  26.4 1.0 gather_fusion
  28.9 25.1 %all-reduce.9.cloned.1.call-done = f32[512,64]{0,1:T(8,128)} async-done(((f32[512,64]{0,1:T(8,128)}), f32[512,64]{0,1:T(8,128)}) %all-reduce.9.cloned.1.call-update) | async-done | bytes 131088 | tf_op jit(solution)/shard_map/psum | solution.py:52
  54.1 90.3 %all-reduce.11.cloned.1.call-done = f32[512,64]{0,1:T(8,128)} async-done(((f32[512,64]{0,1:T(8,128)}), f32[512,64]{0,1:T(8,128)}) %all-reduce.11.cloned.1.call-update) | async-done | bytes 131088 | tf_op jit(solution)/shard_map/psum | solution.py:52
  146.5 1.0 convolution_multiply_fusion.15
  147.9 1.0 convolution_multiply_fusion.14
  148.9 1.3 copy.123
  150.3 1.0 convolution_multiply_fusion.13
  151.3 1.3 copy.125
  152.6 1.0 convolution_multiply_fusion.12
  153.6 1.3 copy.127
  155.0 1.2 fusion.54
  156.3 1.2 convolution_add_fusion.11
  157.5 1.3 convolution_add_fusion.10
  158.8 1.2 convolution_add_fusion.9
  160.8 1.0 gather_fusion.1
  164.1 22.5 %all-reduce.13.cloned.1.call-done = f32[512,64]{0,1:T(8,128)} async-done(((f32[512,64]{0,1:T(8,128)}), f32[512,64]{0,1:T(8,128)}) %all-reduce.13.cloned.1.call-update) | async-done | bytes 131088 | tf_op jit(solution)/shard_map/psum | solution.py:52
  187.1 89.7 %all-reduce.15.cloned.1.call-done = f32[512,64]{0,1:T(8,128)} async-done(((f32[512,64]{0,1:T(8,128)}), f32[512,64]{0,1:T(8,128)}) %all-reduce.15.cloned.1.call-update) | async-done | bytes 131088 | tf_op jit(solution)/shard_map/psum | solution.py:52
  280.5 1.0 convolution_multiply_fusion.11
  281.8 2.0 convolution_multiply_fusion.10
  283.8 1.3 copy.135
  285.1 1.0 convolution_multiply_fusion.9
  286.2 1.3 copy.137
  287.5 1.0 convolution_multiply_fusion.8
  288.5 1.3 copy.139
  289.8 1.2 fusion.49
  291.1 1.3 convolution_add_fusion.8
  292.4 1.2 convolution_add_fusion.7
  293.6 1.2 convolution_add_fusion.6
  295.3 1.0 gather_fusion.2
  299.1 22.0 %all-reduce.17.cloned.1.call-done = f32[512,64]{0,1:T(8,128)} async-done(((f32[512,64]{0,1:T(8,128)}), f32[512,64]{0,1:T(8,128)}) %all-reduce.17.cloned.1.call-update) | async-done | bytes 131088 | tf_op jit(solution)/shard_map/psum | solution.py:52
  321.3 90.0 %all-reduce.19.cloned.1.call-done = f32[512,64]{0,1:T(8,128)} async-done(((f32[512,64]{0,1:T(8,128)}), f32[512,64]{0,1:T(8,128)}) %all-reduce.19.cloned.1.call-update) | async-done | bytes 131088 | tf_op jit(solution)/shard_map/psum | solution.py:52
  414.8 1.0 convolution_multiply_fusion.7
  416.1 1.0 convolution_multiply_fusion.6
  417.2 1.3 copy.147
  418.5 1.0 convolution_multiply_fusion.5
  419.5 1.3 copy.149
  420.9 1.0 convolution_multiply_fusion.4
  421.9 1.3 copy.151
  423.3 1.2 fusion.44
  424.5 1.2 convolution_add_fusion.5
  425.8 1.3 convolution_add_fusion.4
  427.0 1.2 convolution_add_fusion.3
  429.1 1.0 gather_fusion.3
  431.9 22.9 %all-reduce.21.cloned.1.call-done = f32[512,64]{0,1:T(8,128)} async-done(((f32[512,64]{0,1:T(8,128)}), f32[512,64]{0,1:T(8,128)}) %all-reduce.21.cloned.1.call-update) | async-done | bytes 131088 | tf_op jit(solution)/shard_map/psum | solution.py:52
  454.9 90.3 %all-reduce.23.cloned.1.call-done = f32[512,64]{0,1:T(8,128)} async-done(((f32[512,64]{0,1:T(8,128)}), f32[512,64]{0,1:T(8,128)}) %all-reduce.23.cloned.1.call-update) | async-done | bytes 131088 | tf_op jit(solution)/shard_map/psum | solution.py:52
  548.8 1.0 convolution_multiply_fusion.3
  550.2 2.0 convolution_multiply_fusion.2
  552.2 1.3 copy.159
  553.5 1.0 convolution_multiply_fusion.1
  554.5 1.3 copy.161
  555.8 1.0 convolution_multiply_fusion
  556.9 1.3 copy.163
  558.2 1.2 fusion.39
  559.5 1.3 convolution_add_fusion.2
  560.7 1.2 convolution_add_fusion.1
  562.0 1.2 convolution_add_fusion
  563.3 1.1 copy.165
  (190 shorter events, 30.4 us)
Async XLA Ops:
  6.5 47.5 %all-reduce.9.cloned.1.call-start = ((), (), s32[]{:S(2)}) async-start(), calls=%async_computation | async-start | bytes 262144 | tf_op jit(solution)/shard_map/psum | solution.py:52
  7.8 4.4 copy-start.31
  7.9 7.8 %collective-permute-start.1 = (f32[64,4,1]{2,0,1:T(8,128)S(1)}, f32[64,4,1]{2,0,1:T(8,128)S(1)}, u32[]{:S(2)}, u32[]{:S(2)}) collective-permute-start(f32[64,4,1]{2,0,1:T(8,128)S(1)} %get-tuple-element.53), channel_id=1, source_target_pairs={{2,0},{4,2},{6,4},{8,6},{10,8},{12,10},{14,12},{16,14},{18,16},{20... | collective-permute-start | bytes 3080 | tf_op jit(solution)/shard_map/ppermute | solution.py:17
  9.2 6.5 %collective-permute-start = (f32[64,4,1]{2,0,1:T(8,128)S(1)}, f32[64,4,1]{2,0,1:T(8,128)S(1)}, u32[]{:S(2)}, u32[]{:S(2)}) collective-permute-start(f32[64,4,1]{2,0,1:T(8,128)S(1)} %get-tuple-element.52), channel_id=1, source_target_pairs={{0,2},{2,4},{4,6},{6,8},{8,10},{10,12},{12,14},{14,16},{16,18},{18... | collective-permute-start | bytes 3080 | tf_op jit(solution)/shard_map/ppermute | solution.py:15
  12.2 0.7 copy-start.32
  12.9 0.7 copy-start.33
  13.6 0.7 copy-start.34
  14.3 0.7 copy-start.18
  14.3 7.7 %copy-start.16 = (s32[1,512]{1,0:T(1,128)}, s32[1,512]{1,0:T(1,128)S(1)}, u32[]{:S(2)}) copy-start(s32[1,512]{1,0:T(1,128)S(1)} %get-tuple-element.69) | copy-start | bytes 6148
  14.3 0.7 copy-start.37
  14.3 0.7 copy-start.38
  15.8 7.9 %collective-permute-start.3 = (f32[64,1,514]{2,0,1:T(8,128)S(1)}, f32[64,1,514]{2,0,1:T(8,128)S(1)}, u32[]{:S(2)}, u32[]{:S(2)}) collective-permute-start(f32[64,1,514]{2,0,1:T(8,128)S(1)} %get-tuple-element.51), channel_id=1, source_target_pairs={{1,0},{3,2},{5,4},{7,6},{9,8},{11,10},{13,12},{15,14},{17,16},{19,... | collective-permute-start | bytes 394760 | tf_op jit(solution)/shard_map/ppermute | solution.py:17
  17.1 8.4 %collective-permute-start.2 = (f32[64,1,514]{2,0,1:T(8,128)S(1)}, f32[64,1,514]{2,0,1:T(8,128)S(1)}, u32[]{:S(2)}, u32[]{:S(2)}) collective-permute-start(f32[64,1,514]{2,0,1:T(8,128)S(1)} %get-tuple-element.50), channel_id=1, source_target_pairs={{0,1},{2,3},{4,5},{6,7},{8,9},{10,11},{12,13},{14,15},{16,17},{18,... | collective-permute-start | bytes 394760 | tf_op jit(solution)/shard_map/ppermute | solution.py:15
  22.0 3.5 copy-start.23
  22.7 2.9 copy-start.22
  28.3 116.1 %all-reduce.11.cloned.1.call-start = ((), (), s32[]{:S(2)}) async-start(), calls=%async_computation.1 | async-start | bytes 262144 | tf_op jit(solution)/shard_map/psum | solution.py:52
  54.0 132.6 %all-reduce.13.cloned.1.call-start = ((), (), s32[]{:S(2)}) async-start(), calls=%async_computation.2 | async-start | bytes 262144 | tf_op jit(solution)/shard_map/psum | solution.py:52
  144.4 1.0 copy-start.12
  153.6 1.3 copy-start.24
  153.6 1.3 copy-start.25
  155.0 1.3 copy-start
  156.2 1.3 copy-start.4
  157.5 1.3 copy-start.8
  160.1 0.7 copy-start.20
  162.0 0.6 copy-start.49
  162.0 0.7 copy-start.50
  163.3 0.7 copy-start.19
  163.4 0.7 copy-start.36
  163.4 113.4 %all-reduce.15.cloned.1.call-start = ((), (), s32[]{:S(2)}) async-start(), calls=%async_computation.3 | async-start | bytes 262144 | tf_op jit(solution)/shard_map/psum | solution.py:52
  186.6 134.4 %all-reduce.17.cloned.1.call-start = ((), (), s32[]{:S(2)}) async-start(), calls=%async_computation.4 | async-start | bytes 262144 | tf_op jit(solution)/shard_map/psum | solution.py:52
  276.8 1.0 copy-start.13
  277.9 0.7 copy-start.44
  277.9 0.7 copy-start.43
  278.6 0.7 copy-start.30
  289.8 1.3 copy-start.1
  291.1 1.3 copy-start.5
  292.4 1.3 copy-start.9
  296.5 0.6 copy-start.47
  296.5 0.6 copy-start.48
  297.8 0.7 copy-start.17
  297.8 0.7 copy-start.35
  297.8 113.4 %all-reduce.19.cloned.1.call-start = ((), (), s32[]{:S(2)}) async-start(), calls=%async_computation.5 | async-start | bytes 262144 | tf_op jit(solution)/shard_map/psum | solution.py:52
  321.1 133.8 %all-reduce.21.cloned.1.call-start = ((), (), s32[]{:S(2)}) async-start(), calls=%async_computation.6 | async-start | bytes 262144 | tf_op jit(solution)/shard_map/psum | solution.py:52
  411.3 1.0 copy-start.14
  412.3 0.7 copy-start.42
  412.3 0.7 copy-start.41
  413.6 0.7 copy-start.29
  421.9 1.3 copy-start.26
  421.9 1.3 copy-start.27
  423.2 1.3 copy-start.2
  424.5 1.3 copy-start.6
  425.8 1.3 copy-start.10
  428.4 0.7 copy-start.21
  430.2 0.7 copy-start.45
  430.3 0.7 copy-start.46
  431.6 113.6 %all-reduce.23.cloned.1.call-start = ((), (), s32[]{:S(2)}) async-start(), calls=%async_computation.7 | async-start | bytes 262144 | tf_op jit(solution)/shard_map/psum | solution.py:52
  545.2 1.0 copy-start.15
  546.3 0.7 copy-start.40
  546.3 0.7 copy-start.39
  547.0 0.6 copy-start.28
  558.2 1.3 copy-start.3
  559.5 1.3 copy-start.7
  560.7 1.3 copy-start.11
Sparse Core Ops, SparseCore 0:
  28.4 25.5 all-reduce.8
  57.4 86.8 all-reduce.10
  163.5 23.0 all-reduce.12
  189.9 86.8 all-reduce.14
  297.9 23.0 all-reduce.16
  324.3 86.8 all-reduce.18
  431.7 23.0 all-reduce.20
  458.3 86.8 all-reduce.22
